TPU v7x, 512 devices: a whole 4x4x16 slice. The times are simulated.
512 devices in a mesh: dp: 64 (over y, z), group: 8 (over x, core).
Axes of the slice: x: 4, y: 4, z: 16, core: 2. Of those that a mesh axis runs over, the one named last changes fastest.
Arguments:
- queries: bfloat16 [32768, 3200], P(('group', 'dp')), parts along dimension 0, may hold values from -48 to 48
- latent: bfloat16 [32768, 320], P(('group', 'dp')), parts along dimension 0, may hold values from -4 to 4
- cache: bfloat16 [524288, 320], P(('group', 'dp')), parts along dimension 0, may hold values from -4 to 4
- residual: bfloat16 [32768, 1280], P(('group', 'dp')), parts along dimension 0, may hold values from -6 to 6
- value_up: bfloat16 [256, 1280], replicated, may hold values from -0.375 to 0.375
- norm_gain: float32 [1280], replicated, may hold values from 0.5 to 1.5
- cache_lengths: int32 [512], P(('group', 'dp')), parts along dimension 0, may hold values from 1 to 1024, as said below
- routes: int32 [32768, 6], P(('group', 'dp')), parts along dimension 0, may hold values from 0 to 31, all different within a row; in each aligned block of 64 rows (0 to 63, 64 to 127, ...) at most 18 rows name the same one
- route_gates: float32 [32768, 6], P(('group', 'dp')), parts along dimension 0, may hold values from 0.05 to 0.6
- expert_gate: bfloat16 [64, 1280, 384], P('dp'), may hold values from -0.15625 to 0.15625
- expert_up: bfloat16 [64, 1280, 384], P('dp'), may hold values from -0.15625 to 0.15625
- expert_down: bfloat16 [64, 384, 1280], P('dp'), may hold values from -0.21875 to 0.21875
Outputs:
- layer_out: bfloat16 [32768, 1280], P(('group', 'dp')), parts along dimension 0
There are 8 independent parts, one for each index of `group`. A program takes and returns all parts, laid end to end along the dimension named above; an argument that names none is the same for every part. Nothing has to cross between parts.
Inputs may be any that keep to these rules, and one draw needn't show every extreme that they name: `routes`: in the rows of one rank no expert is chosen more than 18 times, and some expert is chosen exactly 18 times on some rank. `cache_lengths`: some rank has exactly 1024 earlier positions.
All inputs are finite; a program needn't handle non-finite values.
Results may differ from a plain program's by a relative error of at most 0.009.
Values may be sent and summed in bfloat16 or wider, within the bound.
No kernel may reach another device: no remote copies, remote signals or barrier semaphores. Data moves between devices by JAX's collectives and lax.ppermute only.
A program may use at most 64 MiB of HBM per device.

v0:
```python
import jax
import jax.numpy as jnp
from jax import lax
from jax.sharding import PartitionSpec as P

HEADS = 10
VHEAD = 128
LATENT = 256
ROPE = 64
TOP = 6


def expert_rows(rows_in, expert_gate, expert_up, expert_down):
    shape_in = rows_in.shape
    flat_rows = rows_in.reshape(-1, shape_in[-1])
    gate = jnp.dot(flat_rows, expert_gate[0], preferred_element_type=jnp.float32)
    upper = jnp.dot(flat_rows, expert_up[0], preferred_element_type=jnp.float32)
    hidden = (jax.nn.silu(gate) * upper).astype(jnp.bfloat16)
    partial_out = jnp.dot(hidden, expert_down[0], preferred_element_type=jnp.float32).astype(
        jnp.bfloat16
    )
    return partial_out.reshape(shape_in)


def on_device(
    queries,
    latent,
    cache,
    residual,
    value_up,
    norm_gain,
    cache_lengths,
    routes,
    route_gates,
    expert_gate,
    expert_up,
    expert_down,
):
    rows_here = queries.shape[0]
    prefix_rows = cache.shape[0]
    stacked = queries.reshape(rows_here, HEADS, LATENT + ROPE)
    keys = jnp.concatenate([cache, latent], axis=0)
    scores = jnp.einsum("thd,sd->hts", stacked, keys, preferred_element_type=jnp.float32) * (
        VHEAD + ROPE
    ) ** (-0.5)
    positions = jnp.arange(rows_here, dtype=jnp.int32)
    key_index = jnp.arange(prefix_rows + rows_here, dtype=jnp.int32)
    from_cache = key_index[None, :] < cache_lengths[0]
    from_new = (key_index[None, :] >= prefix_rows) & (
        key_index[None, :] - prefix_rows <= positions[:, None]
    )
    allowed = from_cache | from_new
    scores = jnp.where(allowed[None], scores, jnp.float32(-1e30))
    largest = jnp.max(scores, axis=2, keepdims=True)
    exponent = jnp.exp(scores - largest)
    attention = (exponent / jnp.sum(exponent, axis=2, keepdims=True)).astype(jnp.bfloat16)
    mixed_latent = jnp.einsum(
        "hts,sr->thr", attention, keys[:, :LATENT], preferred_element_type=jnp.float32
    ).astype(jnp.bfloat16)
    values = jnp.einsum(
        "thr,rhv->thv",
        mixed_latent,
        value_up.reshape(LATENT, HEADS, VHEAD),
        preferred_element_type=jnp.float32,
    ).reshape(rows_here, HEADS * VHEAD)
    middle = (residual.astype(jnp.float32) + values).astype(jnp.bfloat16)
    middle_f = middle.astype(jnp.float32)
    normed = (
        middle_f
        * lax.rsqrt(jnp.mean(middle_f * middle_f, axis=1, keepdims=True) + 1e-06)
        * norm_gain
    ).astype(jnp.bfloat16)
    experts = lax.axis_size("dp") // 2
    capacity = min(rows_here, 3 * rows_here * TOP // (2 * experts))
    width = normed.shape[1]
    flat_routes = routes.reshape(-1)
    onehot = (flat_routes[:, None] == jnp.arange(experts, dtype=jnp.int32)[None, :]).astype(
        jnp.int32
    )
    before = jnp.cumsum(onehot, axis=0) - onehot
    slot_index = jnp.sum(before * onehot, axis=1)
    target = flat_routes * capacity + slot_index
    copies = jnp.repeat(normed, TOP, axis=0)
    buffer = jnp.zeros((experts * capacity, width), jnp.bfloat16).at[target].set(copies)
    buffer = buffer.reshape(experts, capacity, width)
    outgoing = jnp.repeat(buffer, 2, axis=0)
    partials = expert_rows(
        lax.all_to_all(outgoing, "dp", split_axis=0, concat_axis=0, tiled=True),
        expert_gate,
        expert_up,
        expert_down,
    )
    returned = lax.all_to_all(partials, "dp", split_axis=0, concat_axis=0, tiled=True).reshape(
        experts, 2, capacity, width
    )
    finished = (returned[:, 0].astype(jnp.float32) + returned[:, 1].astype(jnp.float32)).astype(
        jnp.bfloat16
    )
    flat_out = finished.reshape(experts * capacity, width)
    picked = flat_out[target].reshape(rows_here, TOP, width).astype(jnp.float32)
    mixture = jnp.sum(route_gates[:, :, None] * picked, axis=1)
    return (middle_f + mixture).astype(jnp.bfloat16)


def solution(mesh):
    return jax.shard_map(
        on_device,
        mesh=mesh,
        in_specs=(
            P(("group", "dp"), None),
            P(("group", "dp"), None),
            P(("group", "dp"), None),
            P(("group", "dp"), None),
            P(),
            P(),
            P(("group", "dp")),
            P(("group", "dp"), None),
            P(("group", "dp"), None),
            P("dp", None, None),
            P("dp", None, None),
            P("dp", None, None),
        ),
        out_specs=P(("group", "dp"), None),
        check_vma=False,
    )
```

profile of v0, /device:TPU:6, one launch (start us, length us, event | category | flops | bytes accessed | tf_op | source)
XLA Modules:
  0.0 438.7 jit_solution(5174371616072524938)
XLA Ops:
  0.0 0.9 copy.26
  0.9 0.1 eq.29
  1.1 0.1 eq.25
  1.2 0.7 broadcast_multiply_fusion
  2.5 0.9 copy.19
  3.5 1.7 reshape.160
  5.1 1.3 copy.21
  6.6 3.2 fusion.54
  9.8 3.0 convolution_bitcast_fusion
  12.8 0.1 fusion.24
  13.0 0.7 copy-done.1
  13.7 0.1 broadcast_in_dim.21
  13.9 0.4 reshape.183
  14.3 0.9 reduce-window.6
  15.1 0.2 slice_reduce_fusion
  15.5 0.1 mul.68
  15.8 3.5 scatter_custom_fusion
  19.3 2.3 reshape.165
  21.6 0.3 broadcast_in_dim.22
  21.9 195.0 %all_to_all.10 = bf16[64,18,1280]{2,1,0:T(8,128)(2,1)} all-to-all(bf16[64,18,1280]{2,1,0:T(8,128)(2,1)S(1)} %bitcast.79), channel_id=1, replica_groups=mesh['dp'=64,'group'=8] {'dp'}, dimensions={0} | all-to-all | bytes 5898240 | tf_op jit(solution)/shard_map/all_to_all | solution.py:88
  216.9 5.6 %reshape.167 = bf16[1152,1280]{1,0:T(8,128)(2,1)} reshape(bf16[64,18,1280]{2,1,0:T(8,128)(2,1)} %all_to_all.10) | data formatting | bytes 5898240 | tf_op jit(solution)/shard_map/reshape | solution.py:15
  222.6 4.8 %fusion.11 = f32[1152,384]{1,0:T(8,128)} fusion(bf16[1152,1280]{1,0:T(8,128)(2,1)} %reshape.167, bf16[1,1280,384]{2,1,0:T(8,128)(2,1)S(1)} %copy-done.6), kind=kOutput, calls=%fused_computation.21 | convolution fusion | flops 1132462080 | bytes 5701632 | tf_op jit(solution)/shard_map/dot_general | solution.py:16
  227.4 7.3 %convolution_convert_fusion = bf16[1152,1280]{1,0:T(8,128)(2,1)} fusion(bf16[1152,1280]{1,0:T(8,128)(2,1)} %reshape.167, f32[1152,384]{1,0:T(8,128)} %fusion.11, bf16[1,384,1280]{2,1,0:T(8,128)(2,1)S(1)} %copy-done, bf16[1,1280,384]{2,1,0:T(8,128)(2,1)S(1)} %copy-done.7), kind=kOutput, calls=%fused_computation.3 | convolution fusion | flops 2269052928 | bytes 9633792 | tf_op jit(solution)/shard_map/dot_general | solution.py:19
  234.7 5.5 %reshape.168 = bf16[64,18,1280]{2,1,0:T(8,128)(2,1)} reshape(bf16[1152,1280]{1,0:T(8,128)(2,1)} %convolution_convert_fusion) | data formatting | bytes 5898240 | tf_op jit(solution)/shard_map/reshape | solution.py:22
  240.2 8.2 %all-to-all-start.1 = ((bf16[64,18,1280]{2,1,0:T(8,128)(2,1)}), bf16[64,18,1280]{2,1,0:T(8,128)(2,1)}, u32[]{:S(2)}, u32[]{:S(2)}) async-start(bf16[64,18,1280]{2,1,0:T(8,128)(2,1)} %reshape.168), calls=%async_computation.1 | async-start | bytes 7864320 | tf_op jit(solution)/shard_map/all_to_all | solution.py:93
  248.5 176.7 %all-to-all-done.1 = bf16[64,18,1280]{2,1,0:T(8,128)(2,1)} async-done(((bf16[64,18,1280]{2,1,0:T(8,128)(2,1)}), bf16[64,18,1280]{2,1,0:T(8,128)(2,1)}, u32[]{:S(2)}, u32[]{:S(2)}) %all-to-all-start.1) | async-done | bytes 2949152 | tf_op jit(solution)/shard_map/all_to_all | solution.py:93
  425.2 3.9 add_convert_fusion
  429.1 2.5 convert_element_type.71
  431.6 2.2 gather_fusion
  433.7 1.6 reshape.170
  435.4 2.6 multiply_reduce_fusion
  438.0 0.7 fusion.27
  (29 shorter events, 0.6 us)
Async XLA Ops:
  0.0 227.4 %copy-start = (bf16[1,384,1280]{2,1,0:T(8,128)(2,1)S(1)}, bf16[1,384,1280]{2,1,0:T(8,128)(2,1)}, u32[]{:S(2)}) copy-start(bf16[1,384,1280]{2,1,0:T(8,128)(2,1)} %param.23) | copy-start | bytes 2949124
  0.0 6.6 %copy-start.8 = (bf16[1024,320]{0,1:T(8,128)(2,1)S(1)}, bf16[1024,320]{0,1:T(8,128)(2,1)}, u32[]{:S(2)}) copy-start(bf16[1024,320]{0,1:T(8,128)(2,1)} %param.14) | copy-start | bytes 1966084
  9.8 3.0 copy-start.3
  9.8 3.8 copy-start.4
  12.9 0.7 copy-start.1
  216.9 5.6 %copy-start.6 = (bf16[1,1280,384]{2,1,0:T(8,128)(2,1)S(1)}, bf16[1,1280,384]{2,1,0:T(8,128)(2,1)}, u32[]{:S(2)}) copy-start(bf16[1,1280,384]{2,1,0:T(8,128)(2,1)} %param.21) | copy-start | bytes 2949124
  222.6 4.9 %copy-start.7 = (bf16[1,1280,384]{2,1,0:T(8,128)(2,1)S(1)}, bf16[1,1280,384]{2,1,0:T(8,128)(2,1)}, u32[]{:S(2)}) copy-start(bf16[1,1280,384]{2,1,0:T(8,128)(2,1)} %param.22) | copy-start | bytes 2949124
  240.2 8.2 %copy-start.5 = (f32[64,6]{0,1:T(8,128)S(1)}, f32[64,6]{0,1:T(8,128)}, u32[]{:S(2)}) copy-start(f32[64,6]{0,1:T(8,128)} %param.20) | copy-start | bytes 4612
  240.2 185.0 %all-to-all-start.1 = ((bf16[64,18,1280]{2,1,0:T(8,128)(2,1)}), bf16[64,18,1280]{2,1,0:T(8,128)(2,1)}, u32[]{:S(2)}, u32[]{:S(2)}) async-start(bf16[64,18,1280]{2,1,0:T(8,128)(2,1)} %reshape.168), calls=%async_computation.1 | async-start | bytes 7864320 | tf_op jit(solution)/shard_map/all_to_all | solution.py:93
  433.7 4.3 copy-start.2
where the time goes:
time: 440 us; the launch traced here: 439 us
  blocking collectives  195 us (44%)
  waiting for transfers between devices  177 us (40%)
  local copies, waits for them, and re-layouts  30.3 us (7%)
  matrix products  18.4 us (4%)
  other arithmetic  9.29 us (2%)
  starting transfers between devices  8.21 us (2%)
    all_to_all x1, blocking collectives, on_device(): lax.all_to_all(outgoing, 'dp', split_axis=0, concat_axis=0, tiled=True)  195 us
    all_to_all x1, waiting for transfers between devices, on_device(): lax.all_to_all(partials, 'dp', split_axis=0, concat_axis=0, tiled=True)  177 us
  transfers between devices with their start and end apart: 1, of which 1 were waited for; matrix products, arithmetic and copies ran while one was open for 0% of the time, Pallas kernels for 0%

commit v1 on v0

v1 whole, which is shorter than its diff:
```python
import jax
import jax.numpy as jnp
import numpy as np
from jax import lax
from jax.sharding import PartitionSpec as P

HEADS = 10
VHEAD = 128
LATENT = 256
ROPE = 64
TOP = 6
NY = 4
NZ = 16
CAP = 18
EXPERTS = 32
EXTRA = 128

FAR = [[y * NZ + 4 * q + r for q in range(4)] for y in range(NY) for r in range(4)]
NEAR = [
    [y * NZ + (2 * k + 1 + s) % NZ for y in range(NY) for s in range(2)] for k in range(NZ // 2)
]
SWAP = [(i, i ^ 1) for i in range(NY * NZ)]


def dot32(a, b):
    return jnp.dot(a, b, preferred_element_type=jnp.float32)


def other_half(weight):
    rows = weight.shape[0] // 8
    mine = lax.dynamic_slice_in_dim(weight, lax.axis_index("group") * rows, rows, axis=0)
    theirs = lax.ppermute(mine, "dp", SWAP)
    return lax.all_gather(theirs, "group", axis=0, tiled=True)


def attend(queries, latent, cache, residual, value_up, norm_gain, cache_lengths):
    rows_here = queries.shape[0]
    prefix_rows = cache.shape[0]
    stacked = queries.reshape(rows_here, HEADS, LATENT + ROPE)
    keys = jnp.concatenate([cache, latent], axis=0)
    scores = jnp.einsum("thd,sd->hts", stacked, keys, preferred_element_type=jnp.float32) * (
        VHEAD + ROPE
    ) ** (-0.5)
    positions = jnp.arange(rows_here, dtype=jnp.int32)
    key_index = jnp.arange(prefix_rows + rows_here, dtype=jnp.int32)
    from_cache = key_index[None, :] < cache_lengths[0]
    from_new = (key_index[None, :] >= prefix_rows) & (
        key_index[None, :] - prefix_rows <= positions[:, None]
    )
    allowed = from_cache | from_new
    scores = jnp.where(allowed[None], scores, jnp.float32(-1e30))
    largest = jnp.max(scores, axis=2, keepdims=True)
    exponent = jnp.exp(scores - largest)
    attention = (exponent / jnp.sum(exponent, axis=2, keepdims=True)).astype(jnp.bfloat16)
    mixed_latent = jnp.einsum(
        "hts,sr->thr", attention, keys[:, :LATENT], preferred_element_type=jnp.float32
    ).astype(jnp.bfloat16)
    values = jnp.einsum(
        "thr,rhv->thv",
        mixed_latent,
        value_up.reshape(LATENT, HEADS, VHEAD),
        preferred_element_type=jnp.float32,
    ).reshape(rows_here, HEADS * VHEAD)
    middle = (residual.astype(jnp.float32) + values).astype(jnp.bfloat16)
    middle_f = middle.astype(jnp.float32)
    normed = (
        middle_f
        * lax.rsqrt(jnp.mean(middle_f * middle_f, axis=1, keepdims=True) + 1e-06)
        * norm_gain
    ).astype(jnp.bfloat16)
    return middle, normed


def gate_columns(routes, route_gates):
    dense = jnp.sum(
        jnp.where(
            routes[:, :, None] == jnp.arange(EXPERTS, dtype=jnp.int32), route_gates[:, :, None], 0.0
        ),
        axis=1,
    )
    high = dense.astype(jnp.bfloat16)
    low = (dense - high.astype(jnp.float32)).astype(jnp.bfloat16)
    pad = jnp.zeros((routes.shape[0], EXTRA - 2 * EXPERTS), jnp.bfloat16)
    return jnp.concatenate([high, low, pad], axis=1)


def select_matrix(gates, near):
    cols = gates.astype(jnp.float32)
    dense = (cols[:, :, :EXPERTS] + cols[:, :, EXPERTS : 2 * EXPERTS]).reshape(-1, EXPERTS)
    member = jnp.arange(8, dtype=jnp.int32)
    expert = (member // 2) * 8 + (near + member % 2) % 8
    pick = (expert[:, None] == jnp.arange(EXPERTS, dtype=jnp.int32)[None, :]).astype(jnp.float32)
    chosen = jnp.einsum("ce,je->jc", dense, pick, precision=lax.Precision.HIGHEST)
    taken = chosen > 0
    ranks = chosen.shape[1] // 64
    counts = jnp.cumsum(taken.reshape(8, ranks, 64).astype(jnp.int32), axis=2) - 1
    slot = counts + CAP * jnp.arange(ranks, dtype=jnp.int32)[None, :, None]
    slot = jnp.where(taken, slot.reshape(8, -1), -1)
    sel = slot[:, None, :] == jnp.arange(CAP * ranks, dtype=jnp.int32)[None, :, None]
    return sel, chosen


def on_device(
    queries,
    latent,
    cache,
    residual,
    value_up,
    norm_gain,
    cache_lengths,
    routes,
    route_gates,
    expert_gate,
    expert_up,
    expert_down,
):
    gate_a, up_a, down_a = expert_gate[0], expert_up[0], expert_down[0]
    gate_b, up_b, down_b = other_half(gate_a), other_half(up_a), other_half(down_a)
    middle, normed = attend(queries, latent, cache, residual, value_up, norm_gain, cache_lengths)
    width = normed.shape[1]
    position = lax.axis_index("dp") % NZ
    near = ((position + NZ - 1) % NZ) // 2

    payload = jnp.concatenate([normed, gate_columns(routes, route_gates)], axis=1)
    spread = jnp.broadcast_to(payload[None], (4,) + payload.shape)
    hub = lax.all_to_all(
        spread, "dp", split_axis=0, concat_axis=0, axis_index_groups=FAR, tiled=True
    )
    sel, chosen = select_matrix(hub[:, :, width:], near)
    outgoing = jnp.einsum(
        "jic,cd->jid",
        sel.astype(jnp.bfloat16),
        hub[:, :, :width].reshape(-1, width),
        preferred_element_type=jnp.float32,
    ).astype(jnp.bfloat16)
    arrived = lax.all_to_all(
        outgoing, "dp", split_axis=0, concat_axis=0, axis_index_groups=NEAR, tiled=True
    ).reshape(-1, width)

    hidden_a = (jax.nn.silu(dot32(arrived, gate_a)) * dot32(arrived, up_a)).astype(jnp.bfloat16)
    hidden_b = (jax.nn.silu(dot32(arrived, gate_b)) * dot32(arrived, up_b)).astype(jnp.bfloat16)
    expert_out = (dot32(hidden_a, down_a) + dot32(hidden_b, down_b)).astype(jnp.bfloat16)
    returned = lax.all_to_all(
        expert_out.reshape(outgoing.shape),
        "dp",
        split_axis=0,
        concat_axis=0,
        axis_index_groups=NEAR,
        tiled=True,
    )
    weight = jnp.where(sel, chosen[:, None, :], 0.0)
    high = weight.astype(jnp.bfloat16)
    low = (weight - high.astype(jnp.float32)).astype(jnp.bfloat16)
    mixed = jnp.einsum("jic,jid->cd", high, returned, preferred_element_type=jnp.float32)
    mixed = mixed + jnp.einsum("jic,jid->cd", low, returned, preferred_element_type=jnp.float32)
    back = lax.all_to_all(
        mixed.astype(jnp.bfloat16).reshape(4, 64, width),
        "dp",
        split_axis=0,
        concat_axis=0,
        axis_index_groups=FAR,
        tiled=True,
    )
    mixture = jnp.sum(back.astype(jnp.float32), axis=0)
    return (middle.astype(jnp.float32) + mixture).astype(jnp.bfloat16)


def solution(mesh):
    return jax.shard_map(
        on_device,
        mesh=mesh,
        in_specs=(
            P(("group", "dp"), None),
            P(("group", "dp"), None),
            P(("group", "dp"), None),
            P(("group", "dp"), None),
            P(),
            P(),
            P(("group", "dp")),
            P(("group", "dp"), None),
            P(("group", "dp"), None),
            P("dp", None, None),
            P("dp", None, None),
            P("dp", None, None),
        ),
        out_specs=P(("group", "dp"), None),
        check_vma=False,
    )
```

time: 440 us -> 216 us (0.49)
  waiting for transfers between devices: 177 us -> 40.5 us
  blocking collectives: 195 us -> 106 us
  local copies, waits for them, and re-layouts: 30.3 us -> 6.43 us
  starting transfers between devices: 8.21 us -> 30 us
  matrix products: 18.4 us -> 26.3 us
  other arithmetic: 9.29 us -> 2.9 us
    all_to_all x1 -> x2, waiting for transfers between devices: 177 us -> 40.5 us  [the longest x1 40.5 us: on_device(): lax.all_to_all(spread, 'dp', split_axis=0, concat_axis=0, axis_index_grou...]
    all_to_all x1 -> x2, blocking collectives: 195 us -> 62.4 us  [the longest x1 35.9 us: on_device(): lax.all_to_all(mixed.astype(jnp.bfloat16).reshape(4, 64, width), 'dp', sp...]
    all_gather x0 -> x3, blocking collectives: none -> 44 us  [other_half(): return lax.all_gather(theirs, 'group', axis=0, tiled=True)]
    reshape x5 -> x1, local copies, waits for them, and re-layouts: 15.5 us -> 0.66 us  [attend(): stacked = queries.reshape(rows_here, HEADS, LATENT + ROPE)]
    all_to_all x1 -> x2, starting transfers between devices: 8.21 us -> 22.2 us  [the longest x1 15.1 us: on_device(): lax.all_to_all(spread, 'dp', split_axis=0, concat_axis=0, axis_index_grou...]
    ppermute x0 -> x3, starting transfers between devices: none -> 7.76 us  [other_half(): theirs = lax.ppermute(mine, 'dp', SWAP)]
    dot_general x3 -> x9, matrix products: 15.1 us -> 22 us  [the longest x4 15.6 us: dot32(): return jnp.dot(a, b, preferred_element_type=jnp.float32)]
  transfers between devices with their start and end apart: 1 -> 5, of which waited for: 1 -> 1; matrix products, arithmetic and copies ran while one was open for 0% -> 1% of each run, Pallas kernels for 0% -> 0%
where the time goes in v1:
time: 216 us; the launch traced here: 214 us
  blocking collectives  106 us (49%)
  waiting for transfers between devices  40.5 us (19%)
  starting transfers between devices  30 us (14%)
  matrix products  26.3 us (12%)
  local copies, waits for them, and re-layouts  6.43 us (3%)
  other arithmetic  2.9 us (1%)
    all_gather x3, blocking collectives, other_half(): return lax.all_gather(theirs, 'group', axis=0, tiled=True)  44 us
    all_to_all x1, waiting for transfers between devices, on_device(): lax.all_to_all(spread, 'dp', split_axis=0, concat_axis=0, axis_index_grou...  40.5 us
    all_to_all x1, blocking collectives, on_device(): lax.all_to_all(mixed.astype(jnp.bfloat16).reshape(4, 64, width), 'dp', sp...  35.9 us
    all_to_all x1, blocking collectives, on_device(): lax.all_to_all(expert_out.reshape(outgoing.shape), 'dp', split_axis=0, co...  26.5 us
    dot_general x4, matrix products, dot32(): return jnp.dot(a, b, preferred_element_type=jnp.float32)  15.6 us
    all_to_all x1, starting transfers between devices, on_device(): lax.all_to_all(spread, 'dp', split_axis=0, concat_axis=0, axis_index_grou...  15.1 us
    ppermute x3, starting transfers between devices, other_half(): theirs = lax.ppermute(mine, 'dp', SWAP)  7.76 us
    all_to_all x1, starting transfers between devices, on_device(): lax.all_to_all(outgoing, 'dp', split_axis=0, concat_axis=0, axis_index_gr...  7.13 us
  transfers between devices with their start and end apart: 5, of which 1 were waited for; matrix products, arithmetic and copies ran while one was open for 1% of the time, Pallas kernels for 0%

profile of v1, /device:TPU:6, one launch (start us, length us, event | category | flops | bytes accessed | tf_op | source)
XLA Modules:
  0.0 213.5 jit_solution(15310364053338114115)
XLA Ops:
  0.8 0.7 select_reduce_fusion
  1.7 0.9 copy.29
  2.6 1.3 copy.32
  4.0 0.7 reshape.155
  4.7 4.3 %fusion.76 = (f32[10,64]{1,0:T(8,128)S(1)}, f32[10,64,1088]{2,1,0:T(8,128)}) fusion(pred[64,1088]{1,0:T(8,128)(4,1)S(1)} %fusion.51, bf16[64,320]{0,1:T(8,128)(2,1)S(1)} %copy.29, bf16[1024,320]{0,1:T(8,128)(2,1)} %param.14, bf16[64,10,320]{2,1,0:T(8,128)(2,1)S(1)} %reshape.155), kind=kOutput, calls=%fused_computation.106 | convolution fusion | flops 449823808 | bytes 3963392 | tf_op jit(solution)/shard_map/sub | solution.py:53
  9.1 3.1 %convolution_bitcast_fusion.2 = f32[10,8,8,128]{3,2,1,0:T(8,128)S(1)} fusion(bf16[256,10,128]{0,2,1:T(8,128)(2,1)S(1)} %bitcast.83, f32[10,64,1088]{2,1,0:T(8,128)} %get-tuple-element.12, f32[10,64]{1,0:T(8,128)S(1)} %get-tuple-element.11, bf16[1024,320]{0,1:T(8,128)(2,1)} %param.14, bf16[64,320]{0,1:T(8,128)(2,1)S(1)} %copy.29), kind=kOutput, calls=%fused_computation.20 | convolution fusion | flops 401129472 | bytes 4467200 | tf_op jit(solution)/shard_map/thr,rhv->thv/dot_general | solution.py:58
  12.2 0.1 fusion.33
  12.6 0.9 broadcast_in_dim.43
  13.5 15.1 %all-to-all-start = ((bf16[4,64,1408]{2,1,0:T(8,128)(2,1)}), bf16[4,64,1408]{2,1,0:T(8,128)(2,1)S(1)}, u32[]{:S(2)}, u32[]{:S(2)}) async-start(bf16[4,64,1408]{2,1,0:T(8,128)(2,1)} %broadcast_in_dim.43), calls=%async_computation | async-start | bytes 1441792 | tf_op jit(solution)/shard_map/all_to_all | solution.py:126
  28.8 40.5 %all-to-all-done = bf16[4,64,1408]{2,1,0:T(8,128)(2,1)S(1)} async-done(((bf16[4,64,1408]{2,1,0:T(8,128)(2,1)}), bf16[4,64,1408]{2,1,0:T(8,128)(2,1)S(1)}, u32[]{:S(2)}, u32[]{:S(2)}) %all-to-all-start) | async-done | bytes 720928 | tf_op jit(solution)/shard_map/all_to_all | solution.py:126
  69.4 0.2 fusion.74
  69.6 0.1 reshape.163
  69.7 0.9 reduce_window_sum.11
  70.8 1.7 convolution_convert_fusion
  72.4 7.1 %all-to-all-start.1 = ((bf16[8,72,1280]{2,1,0:T(8,128)(2,1)}), bf16[8,72,1280]{2,1,0:T(8,128)(2,1)S(1)}, u32[]{:S(2)}, u32[]{:S(2)}) async-start(bf16[8,72,1280]{2,1,0:T(8,128)(2,1)} %convolution_convert_fusion), calls=%async_computation.1 | async-start | bytes 2949120 | tf_op jit(solution)/shard_map/all_to_all | solution.py:136
  79.6 1.9 collective-permute-start.2
  81.5 0.9 dynamic-slice_bitcast_fusion.1
  82.5 3.9 %collective-permute-start.1 = (bf16[160,384]{1,0:T(8,128)(2,1)S(1)}, bf16[160,384]{1,0:T(8,128)(2,1)S(1)}, u32[]{:S(2)}, u32[]{:S(2)}) collective-permute-start(bf16[160,384]{1,0:T(8,128)(2,1)S(1)} %dynamic-slice_bitcast_fusion.1), channel_id=1, source_target_pairs={{0,8},{8,0},{16,24},{24,16},{32,40},{40,32},{48,56},{56,48},{64,72... | collective-permute-start | bytes 368648 | tf_op jit(solution)/shard_map/ppermute | solution.py:32
  86.4 0.9 dynamic-slice_bitcast_fusion.2
  87.3 1.9 collective-permute-start
  89.2 14.7 %all_gather.11 = bf16[384,1280]{1,0:T(8,128)(2,1)} all-gather(bf16[48,1280]{1,0:T(8,128)(2,1)S(1)} %collective-permute-done.2), channel_id=1, replica_groups=mesh['dp'=64,'group'=8] {'group'}, dimensions={0}, use_global_device_ids=true | all-gather | bytes 1105920 | tf_op jit(solution)/shard_map/all_gather | solution.py:33
  103.9 14.7 %all_gather.9 = bf16[1280,384]{1,0:T(8,128)(2,1)} all-gather(bf16[160,384]{1,0:T(8,128)(2,1)S(1)} %collective-permute-done), channel_id=1, replica_groups=mesh['dp'=64,'group'=8] {'group'}, dimensions={0}, use_global_device_ids=true | all-gather | bytes 1105920 | tf_op jit(solution)/shard_map/all_gather | solution.py:33
  118.6 14.7 %all_gather.10 = bf16[1280,384]{1,0:T(8,128)(2,1)} all-gather(bf16[160,384]{1,0:T(8,128)(2,1)S(1)} %collective-permute-done.1), channel_id=1, replica_groups=mesh['dp'=64,'group'=8] {'group'}, dimensions={0}, use_global_device_ids=true | all-gather | bytes 1105920 | tf_op jit(solution)/shard_map/all_gather | solution.py:33
  133.3 3.1 %fusion.15 = f32[576,384]{1,0:T(8,128)} fusion(bf16[576,1280]{1,0:T(8,128)(2,1)S(1)} %bitcast.78, bf16[1,1280,384]{2,1,0:T(8,128)(2,1)} %param.21), kind=kOutput, calls=%fused_computation.23 | convolution fusion | flops 566231040 | bytes 3342336 | tf_op jit(solution)/shard_map/dot_general | solution.py:26
  136.5 1.9 fusion.83
  138.3 4.9 %fusion.11 = f32[576,1280]{1,0:T(8,128)} fusion(bf16[576,1280]{1,0:T(8,128)(2,1)S(1)} %bitcast.80, bf16[1,384,1280]{2,1,0:T(8,128)(2,1)S(1)} %copy-done, bf16[1,1280,384]{2,1,0:T(8,128)(2,1)} %param.22, f32[576,384]{1,0:T(8,128)} %fusion.15), kind=kOutput, calls=%fused_computation.19 | convolution fusion | flops 1133789184 | bytes 7274496 | tf_op jit(solution)/shard_map/dot_general | solution.py:26
  143.2 5.7 %fusion.5 = bf16[576,1280]{1,0:T(8,128)(2,1)} fusion(f32[576,1280]{1,0:T(8,128)} %fusion.11, bf16[384,1280]{1,0:T(8,128)(2,1)} %all_gather.11, f32[576,384]{1,0:T(8,128)} %fusion.83, bf16[576,1280]{1,0:T(8,128)(2,1)S(1)} %bitcast.81, bf16[1280,384]{1,0:T(8,128)(2,1)} %all_gather.10), kind=kOutput, calls=%fused_computation.7 | convolution fusion | flops 1135263744 | bytes 8749056 | tf_op jit(solution)/shard_map/dot_general | solution.py:26
  148.9 26.5 %all_to_all.20 = bf16[8,72,1280]{2,1,0:T(8,128)(2,1)S(1)} all-to-all(bf16[8,72,1280]{2,1,0:T(8,128)(2,1)} %bitcast.82), channel_id=1, replica_groups={{8,16,136,144,264,272,392,400},{24,32,152,160,280,288,408,416},{40,48,1..., dimensions={0} | all-to-all | bytes 2949120 | tf_op jit(solution)/shard_map/all_to_all | solution.py:143
  175.4 0.7 convolution_bitcast_fusion.1
  176.1 0.7 fusion.7
  176.9 35.9 %all_to_all.21 = bf16[4,64,1280]{2,1,0:T(8,128)(2,1)S(1)} all-to-all(bf16[4,64,1280]{2,1,0:T(8,128)(2,1)S(1)} %bitcast.84), channel_id=1, replica_groups={{0,32,64,96},{8,40,72,104},{16,48,80,112},{24,56,88,120},{128,160,192,2..., dimensions={0} | all-to-all | bytes 1310720 | tf_op jit(solution)/shard_map/all_to_all | solution.py:156
  212.8 0.7 fusion.36
  (38 shorter events, 1.1 us)
Async XLA Ops:
  0.0 79.6 %copy-start = (bf16[1,384,1280]{2,1,0:T(8,128)(2,1)S(1)}, bf16[1,384,1280]{2,1,0:T(8,128)(2,1)}, u32[]{:S(2)}) copy-start(bf16[1,384,1280]{2,1,0:T(8,128)(2,1)} %param.23) | copy-start | bytes 2949124
  0.0 4.0 %copy-start.2 = (bf16[64,3200]{1,0:T(8,128)(2,1)S(1)}, bf16[64,3200]{1,0:T(8,128)(2,1)}, u32[]{:S(2)}) copy-start(bf16[64,3200]{1,0:T(8,128)(2,1)} %param.12) | copy-start | bytes 1228804
  9.1 3.1 %copy-start.3 = (bf16[64,1280]{1,0:T(8,128)(2,1)S(1)}, bf16[64,1280]{1,0:T(8,128)(2,1)}, u32[]{:S(2)}) copy-start(bf16[64,1280]{1,0:T(8,128)(2,1)} %param.15) | copy-start | bytes 491524
  9.1 3.3 %copy-start.4 = (f32[1280]{0:T(1024)S(1)}, f32[1280]{0:T(1024)}, u32[]{:S(2)}) copy-start(f32[1280]{0:T(1024)} %param.17) | copy-start | bytes 15364
  13.5 55.8 %all-to-all-start = ((bf16[4,64,1408]{2,1,0:T(8,128)(2,1)}), bf16[4,64,1408]{2,1,0:T(8,128)(2,1)S(1)}, u32[]{:S(2)}, u32[]{:S(2)}) async-start(bf16[4,64,1408]{2,1,0:T(8,128)(2,1)} %broadcast_in_dim.43), calls=%async_computation | async-start | bytes 1441792 | tf_op jit(solution)/shard_map/all_to_all | solution.py:126
  72.4 60.9 %all-to-all-start.1 = ((bf16[8,72,1280]{2,1,0:T(8,128)(2,1)}), bf16[8,72,1280]{2,1,0:T(8,128)(2,1)S(1)}, u32[]{:S(2)}, u32[]{:S(2)}) async-start(bf16[8,72,1280]{2,1,0:T(8,128)(2,1)} %convolution_convert_fusion), calls=%async_computation.1 | async-start | bytes 2949120 | tf_op jit(solution)/shard_map/all_to_all | solution.py:136
  79.6 9.6 %collective-permute-start.2 = (bf16[48,1280]{1,0:T(8,128)(2,1)S(1)}, bf16[48,1280]{1,0:T(8,128)(2,1)S(1)}, u32[]{:S(2)}, u32[]{:S(2)}) collective-permute-start(bf16[48,1280]{1,0:T(8,128)(2,1)S(1)} %dynamic-slice_bitcast_fusion), channel_id=1, source_target_pairs={{0,8},{8,0},{16,24},{24,16},{32,40},{40,32},{48,56},{56,48},{64,72... | collective-permute-start | bytes 368648 | tf_op jit(solution)/shard_map/ppermute | solution.py:32
  82.5 36.2 %collective-permute-start.1 = (bf16[160,384]{1,0:T(8,128)(2,1)S(1)}, bf16[160,384]{1,0:T(8,128)(2,1)S(1)}, u32[]{:S(2)}, u32[]{:S(2)}) collective-permute-start(bf16[160,384]{1,0:T(8,128)(2,1)S(1)} %dynamic-slice_bitcast_fusion.1), channel_id=1, source_target_pairs={{0,8},{8,0},{16,24},{24,16},{32,40},{40,32},{48,56},{56,48},{64,72... | collective-permute-start | bytes 368648 | tf_op jit(solution)/shard_map/ppermute | solution.py:32
  87.3 16.6 %collective-permute-start = (bf16[160,384]{1,0:T(8,128)(2,1)S(1)}, bf16[160,384]{1,0:T(8,128)(2,1)S(1)}, u32[]{:S(2)}, u32[]{:S(2)}) collective-permute-start(bf16[160,384]{1,0:T(8,128)(2,1)S(1)} %dynamic-slice_bitcast_fusion.2), channel_id=1, source_target_pairs={{0,8},{8,0},{16,24},{24,16},{32,40},{40,32},{48,56},{56,48},{64,72... | collective-permute-start | bytes 368648 | tf_op jit(solution)/shard_map/ppermute | solution.py:32
  133.3 3.1 %copy-start.1 = (bf16[1280,384]{1,0:T(8,128)(2,1)S(1)}, bf16[1280,384]{1,0:T(8,128)(2,1)}, u32[]{:S(2)}) copy-start(bf16[1280,384]{1,0:T(8,128)(2,1)} %all_gather.9) | copy-start | bytes 2949124

commit v2 on v0

v2 whole, which is shorter than its diff:
```python
import jax
import jax.numpy as jnp
from jax import lax
from jax.experimental import pallas as pl
from jax.experimental.pallas import tpu as pltpu
from jax.sharding import PartitionSpec as P

HEADS = 10
VHEAD = 128
LATENT = 256
ROPE = 64
KEY = LATENT + ROPE
TOP = 6
NY = 4
NZ = 16
CAP = 18
EXPERTS = 32
EXTRA = 128
GROUP = 8
RANKS = 4
MEMBERS = 8
SLOTS = RANKS * CAP
TOK = 64
D = 1280
FF = 384

FAR = [[y * NZ + 4 * q + r for q in range(4)] for y in range(NY) for r in range(4)]
NEAR = [
    [y * NZ + (2 * k + 1 + s) % NZ for y in range(NY) for s in range(2)] for k in range(NZ // 2)
]
SWAP = [(i, i ^ 1) for i in range(NY * NZ)]

VMEM = pl.BlockSpec(memory_space=pltpu.VMEM)
SMEM = pl.BlockSpec(memory_space=pltpu.SMEM)
ANY = pl.BlockSpec(memory_space=pl.ANY)


def dot32(a, b):
    return jnp.dot(a, b, preferred_element_type=jnp.float32)


def dot_nt(a, b):
    return lax.dot_general(a, b, (((1,), (1,)), ((), ())), preferred_element_type=jnp.float32)


def iota(shape, dim):
    return lax.broadcasted_iota(jnp.int32, shape, dim)


GROWS = D // GROUP
DROWS = FF // GROUP
GBLOCKS = FF // 128
DBLOCKS = D // 128
PACKED = 2 * GBLOCKS * GROWS + DBLOCKS * DROWS


def pack_kernel(mine_ref, gate_ref, up_ref, down_ref, out_ref, sem):
    mine = mine_ref[0]
    copies = []
    at = 0
    for ref, rows, blocks in ((gate_ref, GROWS, GBLOCKS), (up_ref, GROWS, GBLOCKS), (down_ref, DROWS, DBLOCKS)):
        for c in range(blocks):
            copies.append(
                pltpu.make_async_copy(
                    ref.at[mine, :, pl.ds(c * 128, 128)], out_ref.at[pl.ds(at, rows), :], sem.at[len(copies)]
                )
            )
            at += rows
    for copy in copies:
        copy.start()
    for copy in copies:
        copy.wait()


def pack(mine, gate, up, down):
    return pl.pallas_call(
        pack_kernel,
        out_shape=jax.ShapeDtypeStruct((PACKED, 128), jnp.bfloat16),
        in_specs=[SMEM, ANY, ANY, ANY],
        out_specs=ANY,
        scratch_shapes=[pltpu.SemaphoreType.DMA((2 * GBLOCKS + DBLOCKS,))],
        cost_estimate=pl.CostEstimate(flops=0, bytes_accessed=2 * PACKED * 256, transcendentals=0),
        name="pack",
    )(mine, gate.reshape(GROUP, GROWS, FF), up.reshape(GROUP, GROWS, FF), down.reshape(GROUP, DROWS, D))


def attend_kernel(
    length_ref, q_ref, latent_ref, cache_ref, residual_ref, value_up_ref, gain_ref, routes_ref, gates_ref,
    payload_ref, middle_ref, q_s, mid_s,
):
    scale = (VHEAD + ROPE) ** (-0.5)
    for h in range(HEADS):
        q_s[h * TOK : (h + 1) * TOK, :] = q_ref[:, h * KEY : (h + 1) * KEY]
    length = length_ref[0]
    prefix = cache_ref.shape[0]
    bias = jnp.where(iota((1, prefix), 1) < length, 0.0, -1e30).astype(jnp.float32)
    cache = cache_ref[...]
    latent = latent_ref[...]
    step = 2
    causal = iota((step * TOK, TOK), 1) <= iota((step * TOK, TOK), 0) % TOK
    for h in range(0, HEADS, step):
        q = q_s[h * TOK : (h + step) * TOK, :]
        s_old = dot_nt(q, cache) + bias
        s_new = jnp.where(causal, dot_nt(q, latent), -1e30)
        largest = jnp.maximum(
            jnp.max(s_old, axis=1, keepdims=True), jnp.max(s_new, axis=1, keepdims=True)
        )
        e_old = jnp.exp((s_old - largest) * scale)
        e_new = jnp.exp((s_new - largest) * scale)
        total = jnp.sum(e_old, axis=1, keepdims=True) + jnp.sum(e_new, axis=1, keepdims=True)
        mixed = dot32(e_old.astype(jnp.bfloat16), cache[:, :LATENT])
        mixed = mixed + dot32(e_new.astype(jnp.bfloat16), latent[:, :LATENT])
        mixed = (mixed / total).astype(jnp.bfloat16)
        for i in range(step):
            cols = slice((h + i) * VHEAD, (h + i + 1) * VHEAD)
            values = dot32(mixed[i * TOK : (i + 1) * TOK], value_up_ref[:, cols])
            mid_s[:, cols] = (residual_ref[:, cols].astype(jnp.float32) + values).astype(jnp.bfloat16)
    middle = mid_s[...]
    middle_ref[...] = middle
    middle_f = middle.astype(jnp.float32)
    mean = jnp.mean(middle_f * middle_f, axis=1, keepdims=True)
    payload_ref[:, :D] = (middle_f * lax.rsqrt(mean + 1e-06) * gain_ref[...]).astype(jnp.bfloat16)
    lane = iota((TOK, EXTRA), 1)
    dense = jnp.zeros((TOK, EXTRA), jnp.float32)
    for k in range(TOP):
        dense = dense + jnp.where(routes_ref[:, k : k + 1] == lane % EXPERTS, gates_ref[:, k : k + 1], 0.0)
    high = dense.astype(jnp.bfloat16).astype(jnp.float32)
    cols = jnp.where(lane < EXPERTS, high, jnp.where(lane < 2 * EXPERTS, dense - high, 0.0))
    payload_ref[:, D:] = cols.astype(jnp.bfloat16)


def attend(length, queries, latent, cache, residual, value_up, gain, routes, gates):
    return pl.pallas_call(
        attend_kernel,
        out_shape=(
            jax.ShapeDtypeStruct((TOK, D + EXTRA), jnp.bfloat16),
            jax.ShapeDtypeStruct((TOK, D), jnp.bfloat16),
        ),
        in_specs=[SMEM] + [VMEM] * 8,
        out_specs=(VMEM, VMEM),
        scratch_shapes=[
            pltpu.VMEM((HEADS * TOK, KEY), jnp.bfloat16),
            pltpu.VMEM((TOK, D), jnp.bfloat16),
        ],
        compiler_params=pltpu.CompilerParams(vmem_limit_bytes=32 * 1024 * 1024),
        cost_estimate=pl.CostEstimate(flops=900_000_000, bytes_accessed=2_500_000, transcendentals=700_000),
        name="attend",
    )(length, queries, latent, cache, residual, value_up, gain.reshape(1, D), routes, gates)


def expert_of(member, near):
    return (member // 2) * 8 + (near + member % 2) % 8


def select_kernel(near_ref, hub_ref, out_ref):
    near = near_ref[0]
    rows = RANKS * TOK
    hub = hub_ref[...].reshape(rows, D + EXTRA)
    lane = iota((MEMBERS, EXTRA), 1)
    pick = lane == expert_of(iota((MEMBERS, EXTRA), 0), near)
    chosen = dot_nt(pick.astype(jnp.bfloat16), hub[:, D:])
    taken = chosen > 0.0
    first, second = iota((rows, rows), 0), iota((rows, rows), 1)
    upto = (first // TOK == second // TOK) & (first <= second)
    counts = dot32(taken.astype(jnp.bfloat16), upto.astype(jnp.bfloat16)).astype(jnp.int32)
    slot = counts - 1 + CAP * (iota((MEMBERS, rows), 1) // TOK)
    slot = jnp.where(taken, slot, -1)
    sel = slot[:, None, :] == iota((MEMBERS, SLOTS, rows), 1)
    sel = sel.astype(jnp.float32).reshape(MEMBERS * SLOTS, rows).astype(jnp.bfloat16)
    out_ref[...] = dot32(sel, hub[:, :D]).astype(jnp.bfloat16)


def select(near, hub):
    return pl.pallas_call(
        select_kernel,
        out_shape=jax.ShapeDtypeStruct((MEMBERS * SLOTS, D), jnp.bfloat16),
        in_specs=[SMEM, VMEM],
        out_specs=VMEM,
        compiler_params=pltpu.CompilerParams(vmem_limit_bytes=32 * 1024 * 1024),
        cost_estimate=pl.CostEstimate(flops=400_000_000, bytes_accessed=2_300_000, transcendentals=0),
        name="select",
    )(near, hub)


def combine_kernel(near_ref, cols_ref, back_ref, out_ref):
    near = near_ref[0]
    rows = RANKS * TOK
    wide = MEMBERS * SLOTS
    cols = cols_ref[...].reshape(rows, EXTRA)
    lane = iota((EXTRA, wide), 0)
    expert = expert_of(iota((EXTRA, wide), 1) // SLOTS, near)
    high = dot32(cols, (lane == expert).astype(jnp.bfloat16))
    low = dot32(cols, (lane == expert + EXPERTS).astype(jnp.bfloat16))
    taken = (high > 0.0).astype(jnp.bfloat16)
    first, second = iota((rows, rows), 0), iota((rows, rows), 1)
    upto = (first // TOK == second // TOK) & (second <= first)
    counts = dot32(upto.astype(jnp.bfloat16), taken).astype(jnp.int32)
    slot = counts - 1 + CAP * (iota((rows, wide), 0) // TOK)
    here = (slot == iota((rows, wide), 1) % SLOTS) & (high > 0.0)
    back = back_ref[...]
    mixed = dot32(jnp.where(here, high, 0.0).astype(jnp.bfloat16), back)
    mixed = mixed + dot32(jnp.where(here, low, 0.0).astype(jnp.bfloat16), back)
    out_ref[...] = mixed.astype(jnp.bfloat16)


def combine(near, cols, back):
    return pl.pallas_call(
        combine_kernel,
        out_shape=jax.ShapeDtypeStruct((RANKS * TOK, D), jnp.bfloat16),
        in_specs=[SMEM, VMEM, VMEM],
        out_specs=VMEM,
        compiler_params=pltpu.CompilerParams(vmem_limit_bytes=32 * 1024 * 1024),
        cost_estimate=pl.CostEstimate(flops=800_000_000, bytes_accessed=2_300_000, transcendentals=0),
        name="combine",
    )(near, cols, back)


def expert_kernel(x_ref, gate_ref, up_ref, down_ref, other_ref, out_ref, wg, wu, wd, hidden, sem):
    copies = []

    def fetch(src, dst):
        copies.append(pltpu.make_async_copy(src, dst, sem.at[len(copies)]))

    at = 0
    for mine, w in ((gate_ref, wg), (up_ref, wu)):
        fetch(mine, w.at[:, :, pl.ds(0, FF)])
        for c in range(GBLOCKS):
            fetch(other_ref.at[:, pl.ds(at, GROWS), :], w.at[:, :, pl.ds(FF + c * 128, 128)])
            at += GROWS
    first = len(copies)
    fetch(down_ref, wd.at[0])
    for c in range(DBLOCKS):
        fetch(other_ref.at[:, pl.ds(at, DROWS), :], wd.at[1, :, :, pl.ds(c * 128, 128)])
        at += DROWS
    for copy in copies:
        copy.start()
    for copy in copies[:first]:
        copy.wait()
    x = x_ref[...]
    for n in range(0, 2 * FF, 256):
        gate = dot32(x, wg[:, :, n : n + 256].reshape(D, 256))
        upper = dot32(x, wu[:, :, n : n + 256].reshape(D, 256))
        hidden[:, n : n + 256] = (gate / (1.0 + jnp.exp(-gate)) * upper).astype(jnp.bfloat16)
    for copy in copies[first:]:
        copy.wait()
    for n in range(0, D, 256):
        out_ref[:, n : n + 256] = dot32(
            hidden[...], wd[:, :, :, n : n + 256].reshape(2 * FF, 256)
        ).astype(jnp.bfloat16)


def expert(x, gate, up, down, other):
    rows = x.shape[0]
    return pl.pallas_call(
        expert_kernel,
        out_shape=jax.ShapeDtypeStruct((rows, D), jnp.bfloat16),
        in_specs=[VMEM, ANY, ANY, ANY, ANY],
        out_specs=VMEM,
        scratch_shapes=[
            pltpu.VMEM((GROUP, GROWS, 2 * FF), jnp.bfloat16),
            pltpu.VMEM((GROUP, GROWS, 2 * FF), jnp.bfloat16),
            pltpu.VMEM((2, GROUP, DROWS, D), jnp.bfloat16),
            pltpu.VMEM((rows, 2 * FF), jnp.bfloat16),
            pltpu.SemaphoreType.DMA((2 * GBLOCKS + DBLOCKS + 3,)),
        ],
        compiler_params=pltpu.CompilerParams(vmem_limit_bytes=40 * 1024 * 1024),
        cost_estimate=pl.CostEstimate(
            flops=6 * rows * D * 2 * FF, bytes_accessed=9_000_000, transcendentals=rows * 2 * FF
        ),
        name="expert",
    )(
        x,
        gate.reshape(GROUP, GROWS, FF),
        up.reshape(GROUP, GROWS, FF),
        down.reshape(GROUP, DROWS, D),
        other,
    )


def exchange(x, groups):
    return lax.all_to_all(
        x, "dp", split_axis=0, concat_axis=0, axis_index_groups=groups, tiled=True
    )


def on_device(
    queries,
    latent,
    cache,
    residual,
    value_up,
    norm_gain,
    cache_lengths,
    routes,
    route_gates,
    expert_gate,
    expert_up,
    expert_down,
):
    weights = expert_gate[0], expert_up[0], expert_down[0]
    mine = lax.axis_index("group").astype(jnp.int32).reshape(1)
    eighth = lax.ppermute(pack(mine, *weights), "dp", SWAP)
    other = lax.all_gather(eighth, "group", axis=0, tiled=False)

    payload, middle = attend(
        cache_lengths, queries, latent, cache, residual, value_up, norm_gain, routes, route_gates
    )
    position = lax.axis_index("dp") % NZ
    near = (((position + NZ - 1) % NZ) // 2).astype(jnp.int32).reshape(1)
    hub = exchange(jnp.broadcast_to(payload[None], (RANKS,) + payload.shape), FAR)
    outgoing = select(near, hub).reshape(MEMBERS, SLOTS, D)
    arrived = exchange(outgoing, NEAR).reshape(MEMBERS * SLOTS, D)
    finished = expert(arrived, *weights, other).reshape(MEMBERS, SLOTS, D)
    returned = exchange(finished, NEAR).reshape(MEMBERS * SLOTS, D)
    mixed = combine(near, hub[:, :, D:], returned).reshape(RANKS, TOK, D)
    mixture = jnp.sum(exchange(mixed, FAR).astype(jnp.float32), axis=0)
    return (middle.astype(jnp.float32) + mixture).astype(jnp.bfloat16)


def solution(mesh):
    return jax.shard_map(
        on_device,
        mesh=mesh,
        in_specs=(
            P(("group", "dp"), None),
            P(("group", "dp"), None),
            P(("group", "dp"), None),
            P(("group", "dp"), None),
            P(),
            P(),
            P(("group", "dp")),
            P(("group", "dp"), None),
            P(("group", "dp"), None),
            P("dp", None, None),
            P("dp", None, None),
            P("dp", None, None),
        ),
        out_specs=P(("group", "dp"), None),
        check_vma=False,
    )
```

time: 440 us -> 201 us (0.46)
  blocking collectives: 195 us -> 45.7 us
  waiting for transfers between devices: 177 us -> 68.2 us
  starting transfers between devices: 8.21 us -> 35.2 us
  Pallas kernels: 0 us -> 26 us
  local copies, waits for them, and re-layouts: 30.3 us -> 10.1 us
  matrix products: 18.4 us -> 0 us
  between operations: 0.84 us -> 14.3 us
  other arithmetic: 9.29 us -> 0.78 us
    all_to_all x1 -> x3, waiting for transfers between devices: 177 us -> 19.5 us  [exchange(): lax.all_to_all(x, 'dp', split_axis=0, concat_axis=0, axis_index_groups=gr...]
    all_to_all x1, blocking collectives: 195 us -> 45.7 us  [exchange(): lax.all_to_all(x, 'dp', split_axis=0, concat_axis=0, axis_index_groups=gr...]
    pallas_call x0 -> x5, Pallas kernels: none -> 26 us  [the longest x1 12.4 us: pack(): pl.pallas_call(pack_kernel, out_shape=jax.ShapeDtypeStruct((PACKED, 128),...]
    ppermute x0 -> x1, waiting for transfers between devices: none -> 25.1 us  [on_device(): eighth = lax.ppermute(pack(mine, *weights), 'dp', SWAP)]
    all_to_all x1 -> x3, starting transfers between devices: 8.21 us -> 32.3 us  [exchange(): lax.all_to_all(x, 'dp', split_axis=0, concat_axis=0, axis_index_groups=gr...]
    all_gather x0 -> x1, waiting for transfers between devices: none -> 23.6 us  [on_device(): other = lax.all_gather(eighth, 'group', axis=0, tiled=False)]
    dot_general x3 -> x0, matrix products: 15.1 us -> none  [the longest x1 7.31 us: expert_rows(): jnp.dot(hidden, expert_down[0], preferred_element_type=jnp.float32)]
    reshape x5 -> x1, local copies, waits for them, and re-layouts: 15.5 us -> 0.7 us  [attend(): gain.reshape(1, D)]
  transfers between devices with their start and end apart: 1 -> 5, of which waited for: 1 -> 3; matrix products, arithmetic and copies ran while one was open for 0% -> 0% of each run, Pallas kernels for 0% -> 7%
where the time goes in v2:
time: 201 us; the launch traced here: 200 us
  waiting for transfers between devices  68.2 us (34%)
  blocking collectives  45.7 us (23%)
  starting transfers between devices  35.2 us (18%)
  Pallas kernels  26 us (13%)
  between operations  14.3 us (7%)
  local copies, waits for them, and re-layouts  10.1 us (5%)
    all_to_all x1, blocking collectives, exchange(): lax.all_to_all(x, 'dp', split_axis=0, concat_axis=0, axis_index_groups=gr...  45.7 us
    all_to_all x3, starting transfers between devices, exchange(): lax.all_to_all(x, 'dp', split_axis=0, concat_axis=0, axis_index_groups=gr...  32.3 us
    ppermute x1, waiting for transfers between devices, on_device(): eighth = lax.ppermute(pack(mine, *weights), 'dp', SWAP)  25.1 us
    all_gather x1, waiting for transfers between devices, on_device(): other = lax.all_gather(eighth, 'group', axis=0, tiled=False)  23.6 us
    all_to_all x3, waiting for transfers between devices, exchange(): lax.all_to_all(x, 'dp', split_axis=0, concat_axis=0, axis_index_groups=gr...  19.5 us
    pallas_call x1, Pallas kernels, pack(): pl.pallas_call(pack_kernel, out_shape=jax.ShapeDtypeStruct((PACKED, 128),...  12.4 us
    unnamed x25, local copies, waits for them, and re-layouts  8.44 us
    pallas_call x1, Pallas kernels, expert(): pl.pallas_call(expert_kernel, out_shape=jax.ShapeDtypeStruct((rows, D), j...  5.44 us
  transfers between devices with their start and end apart: 5, of which 3 were waited for; matrix products, arithmetic and copies ran while one was open for 0% of the time, Pallas kernels for 7%

profile of v2, /device:TPU:6, one launch (start us, length us, event | category | flops | bytes accessed | tf_op | source)
XLA Modules:
  0.0 200.2 jit_solution(10688351425364595825)
XLA Ops:
  7.3 1.4 copy.13.cache_ref
  8.7 0.7 reshape.25.gain_ref
  9.4 0.8 copy.14.routes_ref
  10.2 0.0 copy-done.10
  10.2 0.1 copy.15.gates_ref
  10.3 0.0 copy-done.6
  10.3 0.0 copy-done.8
  10.4 4.4 %attend.1 = (bf16[64,1408]{1,0:T(8,128)(2,1)S(1)}, bf16[64,1280]{1,0:T(8,128)(2,1)S(1)}) custom-call(s32[1]{0:T(128)S(6)} %copy.16.length_ref, bf16[64,3200]{1,0:T(8,128)(2,1)S(1)} %copy-done.6, bf16[64,320]{1,0:T(8,128)(2,1)S(1)} %copy-done.8, bf16[1024,320]{1,0:T(8,128)(2,1)S(1)} %copy.13.cache_ref, bf16[64,1280]{1,0:T(8,128)(2,1)S(1)} %copy-done.7, ...), custom_call_target="tpu_custom_call" | custom-call | flops 900000000 | bytes 2500000 | tf_op jit(solution)/shard_map/attend/pallas_call | solution.py:133
  14.8 0.9 broadcast_in_dim.2
  15.7 15.1 %all-to-all-start = ((bf16[4,64,1408]{2,1,0:T(8,128)(2,1)}), bf16[4,64,1408]{2,1,0:T(8,128)(2,1)S(1)}, u32[]{:S(2)}, u32[]{:S(2)}) async-start(bf16[4,64,1408]{2,1,0:T(8,128)(2,1)} %broadcast_in_dim.2), calls=%async_computation | async-start | bytes 1441792 | tf_op jit(solution)/shard_map/all_to_all | solution.py:281
  30.7 0.0 all-gather.3.cloned.1.call-start
  30.7 12.4 %pack.1 = bf16[1440,128]{1,0:T(8,128)(2,1)} custom-call(s32[1]{0:T(128)} %bitcast.6.mine_ref, bf16[8,160,384]{2,1,0:T(8,128)(2,1)} %bitcast.14, bf16[8,160,384]{2,1,0:T(8,128)(2,1)} %bitcast.16, bf16[8,48,1280]{2,1,0:T(8,128)(2,1)} %bitcast.18), custom_call_target="tpu_custom_call" | custom-call | bytes 737280 | tf_op jit(solution)/shard_map/pack/pallas_call | solution.py:76
  43.2 2.9 %collective-permute-start = (bf16[1440,128]{1,0:T(8,128)(2,1)}, bf16[1440,128]{1,0:T(8,128)(2,1)S(1)}, u32[]{:S(2)}, u32[]{:S(2)}) collective-permute-start(bf16[1440,128]{1,0:T(8,128)(2,1)} %pack.1), channel_id=1, source_target_pairs={{0,8},{8,0},{16,24},{24,16},{32,40},{40,32},{48,56},{56,48},{64,72... | collective-permute-start | bytes 1105928 | tf_op jit(solution)/shard_map/ppermute | solution.py:302
  46.1 25.1 %collective-permute-done = bf16[1440,128]{1,0:T(8,128)(2,1)S(1)} collective-permute-done((bf16[1440,128]{1,0:T(8,128)(2,1)}, bf16[1440,128]{1,0:T(8,128)(2,1)S(1)}, u32[]{:S(2)}, u32[]{:S(2)}) %collective-permute-start) | collective-permute-done | bytes 368672 | tf_op jit(solution)/shard_map/ppermute | solution.py:302
  71.2 0.8 copy-done.9
  72.0 0.0 all-gather.3.cloned.1.call-update
  72.0 0.0 all-to-all-done.hub_ref
  72.0 1.9 select.9
  73.9 8.9 %all-to-all-start.1 = ((bf16[8,72,1280]{2,1,0:T(8,128)(2,1)}), bf16[8,72,1280]{2,1,0:T(8,128)(2,1)S(1)}, u32[]{:S(2)}, u32[]{:S(2)}) async-start(bf16[8,72,1280]{2,1,0:T(8,128)(2,1)} %bitcast.1), calls=%async_computation.1 | async-start | bytes 2949120 | tf_op jit(solution)/shard_map/all_to_all | solution.py:281
  82.8 23.6 %all-gather.3.cloned.1.call-done = bf16[11520,128]{1,0:T(8,128)(2,1)} async-done(((bf16[1440,128]{1,0:T(8,128)(2,1)}), bf16[11520,128]{1,0:T(8,128)(2,1)}) %all-gather.3.cloned.1.call-update) | async-done | bytes 2949136 | tf_op jit(solution)/shard_map/all_gather | solution.py:303
  106.4 0.0 all-to-all-done.1
  106.4 1.2 copy-done.2
  107.6 1.2 copy-done.3
  108.8 1.8 copy-done.4
  110.7 5.4 %expert.1 = bf16[576,1280]{1,0:T(8,128)(2,1)S(1)} custom-call(bf16[576,1280]{1,0:T(8,128)(2,1)S(1)} %bitcast.11, bf16[8,160,384]{2,1,0:T(8,128)(2,1)S(1)} %bitcast.15, bf16[8,160,384]{2,1,0:T(8,128)(2,1)S(1)} %bitcast.17, bf16[8,48,1280]{2,1,0:T(8,128)(2,1)S(1)} %bitcast.19, bf16[8,1440,128]{2,1,0:T(8,128)(2,1)S(1)} %bitcast.21), custom_call_target="tpu_custom_call" | custom-call | flops 3397386240 | bytes 9000000 | tf_op jit(solution)/shard_map/expert/pallas_call | solution.py:254
  116.1 1.1 copy-done
  117.3 8.3 %all-to-all-start.2 = ((bf16[8,72,1280]{2,1,0:T(8,128)(2,1)}), bf16[8,72,1280]{2,1,0:T(8,128)(2,1)S(1)}, u32[]{:S(2)}, u32[]{:S(2)}) async-start(bf16[8,72,1280]{2,1,0:T(8,128)(2,1)} %bitcast.13), calls=%async_computation.2 | async-start | bytes 2949120 | tf_op jit(solution)/shard_map/all_to_all | solution.py:281
  125.6 19.5 %all-to-all-done.2 = bf16[8,72,1280]{2,1,0:T(8,128)(2,1)S(1)} async-done(((bf16[8,72,1280]{2,1,0:T(8,128)(2,1)}), bf16[8,72,1280]{2,1,0:T(8,128)(2,1)S(1)}, u32[]{:S(2)}, u32[]{:S(2)}) %all-to-all-start.2) | async-done | bytes 1474592 | tf_op jit(solution)/shard_map/all_to_all | solution.py:281
  145.1 1.8 combine.1
  146.9 45.7 %all_to_all.20 = bf16[4,64,1280]{2,1,0:T(8,128)(2,1)S(1)} all-to-all(bf16[4,64,1280]{2,1,0:T(8,128)(2,1)S(1)} %bitcast.20), channel_id=1, replica_groups={{0,32,64,96},{8,40,72,104},{16,48,80,112},{24,56,88,120},{128,160,192,2..., dimensions={0} | all-to-all | bytes 1310720 | tf_op jit(solution)/shard_map/all_to_all | solution.py:281
  192.6 0.1 convert_reduce_fusion
  192.7 0.7 add_convert_fusion
  (15 shorter events, 0.0 us)
Async XLA Ops:
  6.5 3.7 %copy-start.10 = (f32[64,6]{0,1:T(8,128)S(1)}, f32[64,6]{0,1:T(8,128)}, u32[]{:S(2)}) copy-start(f32[64,6]{0,1:T(8,128)} %param.20) | copy-start | bytes 4612
  6.5 3.8 %copy-start.6 = (bf16[64,3200]{1,0:T(8,128)(2,1)S(1)}, bf16[64,3200]{1,0:T(8,128)(2,1)}, u32[]{:S(2)}) copy-start(bf16[64,3200]{1,0:T(8,128)(2,1)} %q_ref.1) | copy-start | bytes 1228804
  6.5 3.8 %copy-start.8 = (bf16[64,320]{1,0:T(8,128)(2,1)S(1)}, bf16[64,320]{1,0:T(8,128)(2,1)}, u32[]{:S(2)}) copy-start(bf16[64,320]{1,0:T(8,128)(2,1)} %latent_ref.1) | copy-start | bytes 122884
  6.5 3.8 %copy-start.7 = (bf16[64,1280]{1,0:T(8,128)(2,1)S(1)}, bf16[64,1280]{1,0:T(8,128)(2,1)}, u32[]{:S(2)}) copy-start(bf16[64,1280]{1,0:T(8,128)(2,1)} %residual_ref.1) | copy-start | bytes 491524
  6.5 3.8 %copy-start.5 = (bf16[256,1280]{1,0:T(8,128)(2,1)S(1)}, bf16[256,1280]{1,0:T(8,128)(2,1)}, u32[]{:S(2)}) copy-start(bf16[256,1280]{1,0:T(8,128)(2,1)} %value_up_ref.1) | copy-start | bytes 1966084
  15.7 56.3 %all-to-all-start = ((bf16[4,64,1408]{2,1,0:T(8,128)(2,1)}), bf16[4,64,1408]{2,1,0:T(8,128)(2,1)S(1)}, u32[]{:S(2)}, u32[]{:S(2)}) async-start(bf16[4,64,1408]{2,1,0:T(8,128)(2,1)} %broadcast_in_dim.2), calls=%async_computation | async-start | bytes 1441792 | tf_op jit(solution)/shard_map/all_to_all | solution.py:281
  30.7 75.7 %all-gather.3.cloned.1.call-start = ((), (), s32[]{:S(2)}) async-start(), calls=%async_computation.4 | async-start | bytes 3317760 | tf_op jit(solution)/shard_map/all_gather | solution.py:303
  43.2 28.1 %collective-permute-start = (bf16[1440,128]{1,0:T(8,128)(2,1)}, bf16[1440,128]{1,0:T(8,128)(2,1)S(1)}, u32[]{:S(2)}, u32[]{:S(2)}) collective-permute-start(bf16[1440,128]{1,0:T(8,128)(2,1)} %pack.1), channel_id=1, source_target_pairs={{0,8},{8,0},{16,24},{24,16},{32,40},{40,32},{48,56},{56,48},{64,72... | collective-permute-start | bytes 1105928 | tf_op jit(solution)/shard_map/ppermute | solution.py:302
  71.2 0.8 copy-start.9
  73.9 32.5 %copy-start.1 = (bf16[1,1280,384]{2,1,0:T(8,128)(2,1)S(1)}, bf16[1,1280,384]{2,1,0:T(8,128)(2,1)}, u32[]{:S(2)}) copy-start(bf16[1,1280,384]{2,1,0:T(8,128)(2,1)} %param.21) | copy-start | bytes 2949124
  73.9 32.5 %all-to-all-start.1 = ((bf16[8,72,1280]{2,1,0:T(8,128)(2,1)}), bf16[8,72,1280]{2,1,0:T(8,128)(2,1)S(1)}, u32[]{:S(2)}, u32[]{:S(2)}) async-start(bf16[8,72,1280]{2,1,0:T(8,128)(2,1)} %bitcast.1), calls=%async_computation.1 | async-start | bytes 2949120 | tf_op jit(solution)/shard_map/all_to_all | solution.py:281
  106.4 1.2 copy-start.2
  107.6 1.2 copy-start.3
  108.8 1.8 copy-start.4
  116.1 1.1 copy-start
  117.3 27.8 %all-to-all-start.2 = ((bf16[8,72,1280]{2,1,0:T(8,128)(2,1)}), bf16[8,72,1280]{2,1,0:T(8,128)(2,1)S(1)}, u32[]{:S(2)}, u32[]{:S(2)}) async-start(bf16[8,72,1280]{2,1,0:T(8,128)(2,1)} %bitcast.13), calls=%async_computation.2 | async-start | bytes 2949120 | tf_op jit(solution)/shard_map/all_to_all | solution.py:281
Sparse Core Ops, SparseCore 0:
  72.1 34.2 all-gather.2

commit v3 on v2

--- a/solution.py
+++ b/solution.py
@@ -32,7 +32,7 @@
 
 VMEM = pl.BlockSpec(memory_space=pltpu.VMEM)
 SMEM = pl.BlockSpec(memory_space=pltpu.SMEM)
-ANY = pl.BlockSpec(memory_space=pl.ANY)
+HBM = pl.BlockSpec(memory_space=pltpu.HBM)
 
 
 def dot32(a, b):
@@ -54,53 +54,57 @@
 PACKED = 2 * GBLOCKS * GROWS + DBLOCKS * DROWS
 
 
-def pack_kernel(mine_ref, gate_ref, up_ref, down_ref, out_ref, sem):
-    mine = mine_ref[0]
-    copies = []
+def pack_kernel(mine_ref, gate_ref, up_ref, down_ref, out_ref):
     at = 0
-    for ref, rows, blocks in ((gate_ref, GROWS, GBLOCKS), (up_ref, GROWS, GBLOCKS), (down_ref, DROWS, DBLOCKS)):
+    for ref, rows, blocks in (
+        (gate_ref, GROWS, GBLOCKS),
+        (up_ref, GROWS, GBLOCKS),
+        (down_ref, DROWS, DBLOCKS),
+    ):
         for c in range(blocks):
-            copies.append(
-                pltpu.make_async_copy(
-                    ref.at[mine, :, pl.ds(c * 128, 128)], out_ref.at[pl.ds(at, rows), :], sem.at[len(copies)]
-                )
-            )
+            out_ref[at : at + rows, :] = ref[0, :, c * 128 : (c + 1) * 128]
             at += rows
-    for copy in copies:
-        copy.start()
-    for copy in copies:
-        copy.wait()
 
 
 def pack(mine, gate, up, down):
+    def slice_of(i, mine_ref):
+        return mine_ref[0], 0, 0
+
     return pl.pallas_call(
         pack_kernel,
         out_shape=jax.ShapeDtypeStruct((PACKED, 128), jnp.bfloat16),
-        in_specs=[SMEM, ANY, ANY, ANY],
-        out_specs=ANY,
-        scratch_shapes=[pltpu.SemaphoreType.DMA((2 * GBLOCKS + DBLOCKS,))],
-        cost_estimate=pl.CostEstimate(flops=0, bytes_accessed=2 * PACKED * 256, transcendentals=0),
+        grid_spec=pltpu.PrefetchScalarGridSpec(
+            num_scalar_prefetch=1,
+            grid=(1,),
+            in_specs=[
+                pl.BlockSpec((1, GROWS, FF), slice_of),
+                pl.BlockSpec((1, GROWS, FF), slice_of),
+                pl.BlockSpec((1, DROWS, D), slice_of),
+            ],
+            out_specs=pl.BlockSpec((PACKED, 128), lambda i, mine_ref: (0, 0)),
+        ),
+        cost_estimate=pl.CostEstimate(flops=0, bytes_accessed=4 * PACKED * 128, transcendentals=0),
         name="pack",
     )(mine, gate.reshape(GROUP, GROWS, FF), up.reshape(GROUP, GROWS, FF), down.reshape(GROUP, DROWS, D))
 
 
 def attend_kernel(
-    length_ref, q_ref, latent_ref, cache_ref, residual_ref, value_up_ref, gain_ref, routes_ref, gates_ref,
+    length_ref, q_ref, latent_ref, cache_t_ref, residual_ref, value_up_ref, gain_ref, routes_t_ref, gates_t_ref,
     payload_ref, middle_ref, q_s, mid_s,
 ):
     scale = (VHEAD + ROPE) ** (-0.5)
     for h in range(HEADS):
         q_s[h * TOK : (h + 1) * TOK, :] = q_ref[:, h * KEY : (h + 1) * KEY]
     length = length_ref[0]
-    prefix = cache_ref.shape[0]
+    prefix = cache_t_ref.shape[1]
     bias = jnp.where(iota((1, prefix), 1) < length, 0.0, -1e30).astype(jnp.float32)
-    cache = cache_ref[...]
+    cache_t = cache_t_ref[...]
     latent = latent_ref[...]
     step = 2
     causal = iota((step * TOK, TOK), 1) <= iota((step * TOK, TOK), 0) % TOK
     for h in range(0, HEADS, step):
         q = q_s[h * TOK : (h + step) * TOK, :]
-        s_old = dot_nt(q, cache) + bias
+        s_old = dot32(q, cache_t) + bias
         s_new = jnp.where(causal, dot_nt(q, latent), -1e30)
         largest = jnp.maximum(
             jnp.max(s_old, axis=1, keepdims=True), jnp.max(s_new, axis=1, keepdims=True)
@@ -108,7 +112,7 @@
         e_old = jnp.exp((s_old - largest) * scale)
         e_new = jnp.exp((s_new - largest) * scale)
         total = jnp.sum(e_old, axis=1, keepdims=True) + jnp.sum(e_new, axis=1, keepdims=True)
-        mixed = dot32(e_old.astype(jnp.bfloat16), cache[:, :LATENT])
+        mixed = dot_nt(e_old.astype(jnp.bfloat16), cache_t[:LATENT, :])
         mixed = mixed + dot32(e_new.astype(jnp.bfloat16), latent[:, :LATENT])
         mixed = (mixed / total).astype(jnp.bfloat16)
         for i in range(step):
@@ -119,14 +123,15 @@
     middle_ref[...] = middle
     middle_f = middle.astype(jnp.float32)
     mean = jnp.mean(middle_f * middle_f, axis=1, keepdims=True)
-    payload_ref[:, :D] = (middle_f * lax.rsqrt(mean + 1e-06) * gain_ref[...]).astype(jnp.bfloat16)
-    lane = iota((TOK, EXTRA), 1)
-    dense = jnp.zeros((TOK, EXTRA), jnp.float32)
+    payload_ref[:, :D] = (middle_f * lax.rsqrt(mean + 1e-06) * gain_ref[...].reshape(1, D)).astype(jnp.bfloat16)
+    row = iota((EXTRA, TOK), 0)
+    dense = jnp.zeros((EXTRA, TOK), jnp.float32)
     for k in range(TOP):
-        dense = dense + jnp.where(routes_ref[:, k : k + 1] == lane % EXPERTS, gates_ref[:, k : k + 1], 0.0)
+        dense = dense + jnp.where(routes_t_ref[k : k + 1, :] == row % EXPERTS, gates_t_ref[k : k + 1, :], 0.0)
     high = dense.astype(jnp.bfloat16).astype(jnp.float32)
-    cols = jnp.where(lane < EXPERTS, high, jnp.where(lane < 2 * EXPERTS, dense - high, 0.0))
-    payload_ref[:, D:] = cols.astype(jnp.bfloat16)
+    rows = jnp.where(row < EXPERTS, high, jnp.where(row < 2 * EXPERTS, dense - high, 0.0))
+    same = (iota((TOK, TOK), 0) == iota((TOK, TOK), 1)).astype(jnp.bfloat16)
+    payload_ref[:, D:] = dot_nt(same, rows.astype(jnp.bfloat16)).astype(jnp.bfloat16)
 
 
 def attend(length, queries, latent, cache, residual, value_up, gain, routes, gates):
@@ -145,7 +150,7 @@
         compiler_params=pltpu.CompilerParams(vmem_limit_bytes=32 * 1024 * 1024),
         cost_estimate=pl.CostEstimate(flops=900_000_000, bytes_accessed=2_500_000, transcendentals=700_000),
         name="attend",
-    )(length, queries, latent, cache, residual, value_up, gain.reshape(1, D), routes, gates)
+    )(length, queries, latent, cache.T, residual, value_up, gain, routes.T, gates.T)
 
 
 def expert_of(member, near):
@@ -215,7 +220,7 @@
     )(near, cols, back)
 
 
-def expert_kernel(x_ref, gate_ref, up_ref, down_ref, other_ref, out_ref, wg, wu, wd, hidden, sem):
+def expert_kernel(x_ref, gate_ref, up_ref, down_ref, other_ref, out_ref, wg, wu, wd, hidden, done, sem):
     copies = []
 
     def fetch(src, dst):
@@ -243,10 +248,17 @@
         hidden[:, n : n + 256] = (gate / (1.0 + jnp.exp(-gate)) * upper).astype(jnp.bfloat16)
     for copy in copies[first:]:
         copy.wait()
-    for n in range(0, D, 256):
-        out_ref[:, n : n + 256] = dot32(
-            hidden[...], wd[:, :, :, n : n + 256].reshape(2 * FF, 256)
-        ).astype(jnp.bfloat16)
+    sends = []
+    for i, n in enumerate(range(0, D, 256)):
+        done[i] = dot32(hidden[...], wd[:, :, :, n : n + 256].reshape(2 * FF, 256)).astype(jnp.bfloat16)
+        sends.append(
+            pltpu.make_async_copy(
+                done.at[i], out_ref.at[:, pl.ds(n, 256)], sem.at[len(copies) + i]
+            )
+        )
+        sends[-1].start()
+    for send in sends:
+        send.wait()
 
 
 def expert(x, gate, up, down, other):
@@ -254,16 +266,17 @@
     return pl.pallas_call(
         expert_kernel,
         out_shape=jax.ShapeDtypeStruct((rows, D), jnp.bfloat16),
-        in_specs=[VMEM, ANY, ANY, ANY, ANY],
-        out_specs=VMEM,
+        in_specs=[VMEM, HBM, HBM, HBM, HBM],
+        out_specs=HBM,
         scratch_shapes=[
             pltpu.VMEM((GROUP, GROWS, 2 * FF), jnp.bfloat16),
             pltpu.VMEM((GROUP, GROWS, 2 * FF), jnp.bfloat16),
             pltpu.VMEM((2, GROUP, DROWS, D), jnp.bfloat16),
             pltpu.VMEM((rows, 2 * FF), jnp.bfloat16),
-            pltpu.SemaphoreType.DMA((2 * GBLOCKS + DBLOCKS + 3,)),
+            pltpu.VMEM((D // 256, rows, 256), jnp.bfloat16),
+            pltpu.SemaphoreType.DMA((2 * GBLOCKS + DBLOCKS + 3 + D // 256,)),
         ],
-        compiler_params=pltpu.CompilerParams(vmem_limit_bytes=40 * 1024 * 1024),
+        compiler_params=pltpu.CompilerParams(vmem_limit_bytes=60 * 1024 * 1024),
         cost_estimate=pl.CostEstimate(
             flops=6 * rows * D * 2 * FF, bytes_accessed=9_000_000, transcendentals=rows * 2 * FF
         ),
@@ -299,16 +312,18 @@
 ):
     weights = expert_gate[0], expert_up[0], expert_down[0]
     mine = lax.axis_index("group").astype(jnp.int32).reshape(1)
-    eighth = lax.ppermute(pack(mine, *weights), "dp", SWAP)
-    other = lax.all_gather(eighth, "group", axis=0, tiled=False)
-
+    packed, queries = lax.optimization_barrier((pack(mine, *weights), queries))
+    eighth = lax.ppermute(packed, "dp", SWAP)
     payload, middle = attend(
         cache_lengths, queries, latent, cache, residual, value_up, norm_gain, routes, route_gates
     )
+    eighth, payload = lax.optimization_barrier((eighth, payload))
+    other = lax.all_gather(eighth, "group", axis=0, tiled=False)
     position = lax.axis_index("dp") % NZ
     near = (((position + NZ - 1) % NZ) // 2).astype(jnp.int32).reshape(1)
-    hub = exchange(jnp.broadcast_to(payload[None], (RANKS,) + payload.shape), FAR)
+    hub = lax.all_gather(payload, "dp", axis=0, axis_index_groups=FAR, tiled=False)
     outgoing = select(near, hub).reshape(MEMBERS, SLOTS, D)
+    outgoing, other = lax.optimization_barrier((outgoing, other))
     arrived = exchange(outgoing, NEAR).reshape(MEMBERS * SLOTS, D)
     finished = expert(arrived, *weights, other).reshape(MEMBERS, SLOTS, D)
     returned = exchange(finished, NEAR).reshape(MEMBERS * SLOTS, D)

time: 201 us -> 176 us (0.88)
  blocking collectives: 45.7 us -> 109 us
  waiting for transfers between devices: 68.2 us -> 21.8 us
  starting transfers between devices: 35.2 us -> 9.76 us
  local copies, waits for them, and re-layouts: 10.1 us -> 0.8 us
  Pallas kernels: 26 us -> 18.1 us
    all_gather x0 -> x1, blocking collectives: none -> 38.4 us  [on_device(): lax.all_gather(payload, 'dp', axis=0, axis_index_groups=FAR, tiled=False)]
    all_to_all x3 -> x1, starting transfers between devices: 32.3 us -> 5.94 us  [exchange(): lax.all_to_all(x, 'dp', split_axis=0, concat_axis=0, axis_index_groups=gr...]
    all_to_all x1 -> x2, blocking collectives: 45.7 us -> 70.4 us  [exchange(): lax.all_to_all(x, 'dp', split_axis=0, concat_axis=0, axis_index_groups=gr...]
    all_gather x1, waiting for transfers between devices: 23.6 us -> 0.02 us  [on_device(): other = lax.all_gather(eighth, 'group', axis=0, tiled=False)]
    ppermute x1, waiting for transfers between devices: 25.1 us -> 3.18 us  [on_device(): eighth = lax.ppermute(packed, 'dp', SWAP)]
    pallas_call x1, Pallas kernels: 12.4 us -> 1.95 us  [pack(): pl.pallas_call(pack_kernel, out_shape=jax.ShapeDtypeStruct((PACKED, 128),...]
    unnamed x25 -> x18, local copies, waits for them, and re-layouts: 8.44 us -> 0.78 us
    pallas_call x1, Pallas kernels: 5.44 us -> 8.63 us  [expert(): pl.pallas_call(expert_kernel, out_shape=jax.ShapeDtypeStruct((rows, D), j...]
  transfers between devices with their start and end apart: 5 -> 3, of which waited for: 3 -> 2; matrix products, arithmetic and copies ran while one was open for 0% -> 0% of each run, Pallas kernels for 7% -> 3%
where the time goes in v3:
time: 176 us; the launch traced here: 174 us
  blocking collectives  109 us (62%)
  waiting for transfers between devices  21.8 us (12%)
  Pallas kernels  18.1 us (10%)
  between operations  14.2 us (8%)
  starting transfers between devices  9.76 us (6%)
    all_to_all x2, blocking collectives, exchange(): lax.all_to_all(x, 'dp', split_axis=0, concat_axis=0, axis_index_groups=gr...  70.4 us
    all_gather x1, blocking collectives, on_device(): lax.all_gather(payload, 'dp', axis=0, axis_index_groups=FAR, tiled=False)  38.4 us
    all_to_all x1, waiting for transfers between devices, exchange(): lax.all_to_all(x, 'dp', split_axis=0, concat_axis=0, axis_index_groups=gr...  18.6 us
    pallas_call x1, Pallas kernels, expert(): pl.pallas_call(expert_kernel, out_shape=jax.ShapeDtypeStruct((rows, D), j...  8.63 us
    all_to_all x1, starting transfers between devices, exchange(): lax.all_to_all(x, 'dp', split_axis=0, concat_axis=0, axis_index_groups=gr...  5.94 us
    pallas_call x1, Pallas kernels, attend(): pl.pallas_call(attend_kernel, out_shape=(jax.ShapeDtypeStruct((TOK, D + E...  4.87 us
    ppermute x1, starting transfers between devices, on_device(): eighth = lax.ppermute(packed, 'dp', SWAP)  3.81 us
  transfers between devices with their start and end apart: 3, of which 2 were waited for; matrix products, arithmetic and copies ran while one was open for 0% of the time, Pallas kernels for 3%

profile of v3, /device:TPU:6, one launch (start us, length us, event | category | flops | bytes accessed | tf_op | source)
XLA Modules:
  0.0 174.3 jit_solution(9646974283505325952)
XLA Ops:
  6.5 0.0 all-gather.4.cloned.1.call-start
  6.5 0.0 copy-start
  6.5 0.0 copy-start.1
  6.5 0.0 copy-start.4
  6.6 0.0 copy-start.5
  6.6 0.0 copy-start.6
  6.6 0.0 copy-start.7
  6.6 1.9 %pack.1 = bf16[1440,128]{1,0:T(8,128)(2,1)} custom-call(s32[1]{0:T(128)} %bitcast.mine_ref, bf16[8,160,384]{2,1,0:T(8,128)(2,1)} %bitcast.25, bf16[8,160,384]{2,1,0:T(8,128)(2,1)} %bitcast.27, bf16[8,48,1280]{2,1,0:T(8,128)(2,1)} %bitcast.29), custom_call_target="tpu_custom_call" | custom-call | bytes 737280 | tf_op jit(solution)/shard_map/pack/pallas_call | solution.py:73
  8.5 3.8 %collective-permute-start = (bf16[1440,128]{1,0:T(8,128)(2,1)}, bf16[1440,128]{1,0:T(8,128)(2,1)S(1)}, u32[]{:S(2)}, u32[]{:S(2)}) collective-permute-start(bf16[1440,128]{1,0:T(8,128)(2,1)} %pack.1), channel_id=1, source_target_pairs={{0,8},{8,0},{16,24},{24,16},{32,40},{40,32},{48,56},{56,48},{64,72... | collective-permute-start | bytes 1105928 | tf_op jit(solution)/shard_map/ppermute | solution.py:316
  13.0 0.0 copy-done
  13.0 0.0 copy-done.1
  13.0 0.0 copy-done.2
  13.0 0.0 copy-done.3
  13.0 0.0 copy-done.4
  13.1 0.0 copy-done.5
  13.1 0.0 copy-done.6
  13.1 0.0 copy-done.7
  13.1 4.9 %attend.1 = (bf16[64,1408]{1,0:T(8,128)(2,1)S(1)}, bf16[64,1280]{1,0:T(8,128)(2,1)S(1)}) custom-call(s32[1]{0:T(128)S(6)} %copy.13.length_ref, bf16[64,3200]{1,0:T(8,128)(2,1)S(1)} %copy-done.2, bf16[64,320]{1,0:T(8,128)(2,1)S(1)} %copy-done.4, bf16[320,1024]{1,0:T(8,128)(2,1)S(1)} %bitcast.20, bf16[64,1280]{1,0:T(8,128)(2,1)S(1)} %copy-done.3, ...), custom_call_target="tpu_custom_call" | custom-call | flops 900000000 | bytes 2500000 | tf_op jit(solution)/shard_map/attend/pallas_call | solution.py:138
  18.0 3.2 %collective-permute-done = bf16[1440,128]{1,0:T(8,128)(2,1)S(1)} collective-permute-done((bf16[1440,128]{1,0:T(8,128)(2,1)}, bf16[1440,128]{1,0:T(8,128)(2,1)S(1)}, u32[]{:S(2)}, u32[]{:S(2)}) %collective-permute-start) | collective-permute-done | bytes 368672 | tf_op jit(solution)/shard_map/ppermute | solution.py:316
  21.1 0.8 copy-done.8
  21.9 0.0 all-gather.4.cloned.1.call-update
  22.0 38.4 %all-gather = bf16[256,1408]{1,0:T(8,128)(2,1)S(1)} all-gather(bf16[64,1408]{1,0:T(8,128)(2,1)S(1)} %get-tuple-element.17), channel_id=2, replica_groups={{0,32,64,96},{8,40,72,104},{16,48,80,112},{24,56,88,120},{128,160,192,2..., dimensions={0}, use_global_device_ids=true | all-gather | bytes 901120 | tf_op jit(solution)/shard_map/all_gather | solution.py:324
  60.4 0.8 select.9
  61.2 0.0 all-gather.4.cloned.1.call-done
  61.2 26.5 %all_to_all.15 = bf16[8,72,1280]{2,1,0:T(8,128)(2,1)} all-to-all(bf16[8,72,1280]{2,1,0:T(8,128)(2,1)S(1)} %bitcast.15), channel_id=1, replica_groups={{8,16,136,144,264,272,392,400},{24,32,152,160,280,288,408,416},{40,48,1..., dimensions={0} | all-to-all | bytes 2949120 | tf_op jit(solution)/shard_map/all_to_all | solution.py:294
  87.7 8.6 %expert.1 = bf16[576,1280]{1,0:T(8,128)(2,1)} custom-call(bf16[576,1280]{1,0:T(8,128)(2,1)} %bitcast.24, bf16[8,160,384]{2,1,0:T(8,128)(2,1)} %bitcast.26, bf16[8,160,384]{2,1,0:T(8,128)(2,1)} %bitcast.28, bf16[8,48,1280]{2,1,0:T(8,128)(2,1)} %bitcast.30, bf16[8,1440,128]{2,1,0:T(8,128)(2,1)} %bitcast.31), custom_call_target="tpu_custom_call" | custom-call | flops 3397386240 | bytes 9000000 | tf_op jit(solution)/shard_map/expert/pallas_call | solution.py:266
  96.4 5.9 %all-to-all-start.1 = ((bf16[8,72,1280]{2,1,0:T(8,128)(2,1)}), bf16[8,72,1280]{2,1,0:T(8,128)(2,1)S(1)}, u32[]{:S(2)}, u32[]{:S(2)}) async-start(bf16[8,72,1280]{2,1,0:T(8,128)(2,1)} %bitcast.23), calls=%async_computation.1 | async-start | bytes 2949120 | tf_op jit(solution)/shard_map/all_to_all | solution.py:294
  102.3 18.6 %all-to-all-done.1 = bf16[8,72,1280]{2,1,0:T(8,128)(2,1)S(1)} async-done(((bf16[8,72,1280]{2,1,0:T(8,128)(2,1)}), bf16[8,72,1280]{2,1,0:T(8,128)(2,1)S(1)}, u32[]{:S(2)}, u32[]{:S(2)}) %all-to-all-start.1) | async-done | bytes 1474592 | tf_op jit(solution)/shard_map/all_to_all | solution.py:294
  120.9 1.8 %combine.1 = bf16[256,1280]{1,0:T(8,128)(2,1)S(1)} custom-call(s32[1]{0:T(128)} %bitcast.7.near_ref, bf16[4,64,128]{2,1,0:T(8,128)(2,1)S(1)} %slice.4.cols_ref, bf16[576,1280]{1,0:T(8,128)(2,1)S(1)} %bitcast.18), custom_call_target="tpu_custom_call" | custom-call | flops 800000000 | bytes 2300000 | tf_op jit(solution)/shard_map/combine/pallas_call | solution.py:212
  122.7 43.9 %all_to_all.16 = bf16[4,64,1280]{2,1,0:T(8,128)(2,1)S(1)} all-to-all(bf16[4,64,1280]{2,1,0:T(8,128)(2,1)S(1)} %bitcast.19), channel_id=1, replica_groups={{0,32,64,96},{8,40,72,104},{16,48,80,112},{24,56,88,120},{128,160,192,2..., dimensions={0} | all-to-all | bytes 1310720 | tf_op jit(solution)/shard_map/all_to_all | solution.py:294
  166.7 0.1 convert_reduce_fusion
  166.7 0.7 add_convert_fusion
  (4 shorter events, 0.0 us)
Async XLA Ops:
  6.5 54.7 %all-gather.4.cloned.1.call-start = ((), (), s32[]{:S(2)}) async-start(), calls=%async_computation.3 | async-start | bytes 3317760 | tf_op jit(solution)/shard_map/all_gather | solution.py:321
  6.5 6.5 %copy-start = (bf16[1024,320]{0,1:T(8,128)(2,1)S(1)}, bf16[1024,320]{0,1:T(8,128)(2,1)}, u32[]{:S(2)}) copy-start(bf16[1024,320]{0,1:T(8,128)(2,1)} %param.14) | copy-start | bytes 1966084
  6.5 6.5 %copy-start.1 = (bf16[256,1280]{1,0:T(8,128)(2,1)S(1)}, bf16[256,1280]{1,0:T(8,128)(2,1)}, u32[]{:S(2)}) copy-start(bf16[256,1280]{1,0:T(8,128)(2,1)} %value_up_ref.1) | copy-start | bytes 1966084
  6.5 6.5 %copy-start.2 = (bf16[64,3200]{1,0:T(8,128)(2,1)S(1)}, bf16[64,3200]{1,0:T(8,128)(2,1)}, u32[]{:S(2)}) copy-start(bf16[64,3200]{1,0:T(8,128)(2,1)} %q_ref) | copy-start | bytes 1228804
  6.5 6.5 %copy-start.3 = (bf16[64,1280]{1,0:T(8,128)(2,1)S(1)}, bf16[64,1280]{1,0:T(8,128)(2,1)}, u32[]{:S(2)}) copy-start(bf16[64,1280]{1,0:T(8,128)(2,1)} %residual_ref.1) | copy-start | bytes 491524
  6.5 6.5 %copy-start.4 = (bf16[64,320]{1,0:T(8,128)(2,1)S(1)}, bf16[64,320]{1,0:T(8,128)(2,1)}, u32[]{:S(2)}) copy-start(bf16[64,320]{1,0:T(8,128)(2,1)} %latent_ref.1) | copy-start | bytes 122884
  6.6 6.5 %copy-start.5 = (f32[1280]{0:T(1024)S(1)}, f32[1280]{0:T(1024)}, u32[]{:S(2)}) copy-start(f32[1280]{0:T(1024)} %gain_ref.1) | copy-start | bytes 15364
  6.6 6.5 %copy-start.6 = (s32[64,6]{0,1:T(8,128)S(1)}, s32[64,6]{0,1:T(8,128)}, u32[]{:S(2)}) copy-start(s32[64,6]{0,1:T(8,128)} %param.19) | copy-start | bytes 4612
  6.6 6.5 %copy-start.7 = (f32[64,6]{0,1:T(8,128)S(1)}, f32[64,6]{0,1:T(8,128)}, u32[]{:S(2)}) copy-start(f32[64,6]{0,1:T(8,128)} %param.20) | copy-start | bytes 4612
  8.5 12.6 %collective-permute-start = (bf16[1440,128]{1,0:T(8,128)(2,1)}, bf16[1440,128]{1,0:T(8,128)(2,1)S(1)}, u32[]{:S(2)}, u32[]{:S(2)}) collective-permute-start(bf16[1440,128]{1,0:T(8,128)(2,1)} %pack.1), channel_id=1, source_target_pairs={{0,8},{8,0},{16,24},{24,16},{32,40},{40,32},{48,56},{56,48},{64,72... | collective-permute-start | bytes 1105928 | tf_op jit(solution)/shard_map/ppermute | solution.py:316
  21.1 0.8 copy-start.8
  96.4 24.5 %all-to-all-start.1 = ((bf16[8,72,1280]{2,1,0:T(8,128)(2,1)}), bf16[8,72,1280]{2,1,0:T(8,128)(2,1)S(1)}, u32[]{:S(2)}, u32[]{:S(2)}) async-start(bf16[8,72,1280]{2,1,0:T(8,128)(2,1)} %bitcast.23), calls=%async_computation.1 | async-start | bytes 2949120 | tf_op jit(solution)/shard_map/all_to_all | solution.py:294
Sparse Core Ops, SparseCore 0:
  22.0 37.9 all-gather.3
